TPU v7x, 128 devices: a whole 4x4x4 slice. The times are simulated.
128 devices in a mesh: lon: 16 (over y_lo, z, core), lat: 8 (over x, y_hi).
Axes of the slice: x: 4, y: 4 (y_hi: 2, y_lo: 2; y = y_hi * 2 + y_lo), z: 4, core: 2. Of those that a mesh axis runs over, the one named last changes fastest.
Arguments:
- fields: bfloat16 [2, 4, 48, 384, 192], P(None, None, 'lat', 'lon'), may hold values from -6 to 6
- merge_cotangent: bfloat16 [192, 2, 4, 24, 384], P(None, None, None, 'lat', 'lon'), may hold values from -6 to 6
- attend_gain: float32 [192], replicated, may hold values from 0.1 to 1.9
- triple_weight: bfloat16 [192, 576], replicated, may hold values from -0.4375 to 0.4375
- bias_table: float32 [8, 2, 6, 3312], P('lat'), may hold values from -320 to 320
- output_weight: bfloat16 [192, 192], replicated, may hold values from -0.4375 to 0.4375
- feed_gain: float32 [192], replicated, may hold values from 0.1 to 1.9
- expand_weight: bfloat16 [192, 768], replicated, may hold values from -0.4375 to 0.4375
- shrink_weight: bfloat16 [768, 192], replicated, may hold values from -0.21875 to 0.21875
- merge_gain: float32 [768], replicated, may hold values from 0.1 to 1.9
- merge_weight: bfloat16 [768, 384], P(None, 'lon'), may hold values from -0.21875 to 0.21875
Outputs:
- grad_fields: bfloat16 [2, 4, 48, 384, 192], P(None, None, 'lat', 'lon')
- grad_triple: float32 [192, 576], replicated
- grad_output: float32 [192, 192], replicated
- grad_expand: float32 [192, 768], replicated
- grad_shrink: float32 [768, 192], replicated
- grad_attend_gain: float32 [192], replicated
- grad_feed_gain: float32 [192], replicated
- grad_table: float32 [8, 2, 6, 3312], P('lat')
All inputs are finite; a program needn't handle non-finite values.
Results may differ from a plain program's by a relative error of at most 0.035.
Values may be sent and summed in bfloat16 or wider, within the bound.
A program may use at most 128 MiB of HBM per device.

v0:
```python
import functools
import math

import jax
import jax.numpy as jnp
import numpy as np
from jax import lax
from jax.experimental import pallas as pl
from jax.experimental.pallas import tpu as pltpu
from jax.sharding import PartitionSpec as P

F32 = jnp.float32
BF16 = jnp.bfloat16
I32 = jnp.int32
MESH = pl.DeviceIdType.MESH

EPS = 1e-05
MASKED = -1000000000.0
NLON = 16
NLAT = 8
NCHIP = 8
C = 192
HEADS = 6
FF = 768
WIN = 144
NWIN = 8
TOK = WIN * NWIN
HALF = TOK // 2
SIZES = ((216, 112), (72, 40), (72, 40))
POS = 3312
CHUNK = 288
NCHUNK = TOK // CHUNK
TILE = 48
WIDE = 896
FACTOR = 32 ** -0.5


def order_indices():
    natural_to_quad = np.full(640, -1, np.int32)
    quad_to_natural = np.full(640, -1, np.int32)
    quad_to_window = np.full(640, -1, np.int32)
    window_to_quad = np.full(640, -1, np.int32)
    for level in range(4):
        for row in range(6):
            for col in range(24):
                source = (level * 6 + row) * 24 + col
                if col >= 6:
                    place = (0 if row >= 3 else 216) + level * 54 + (row % 3) * 18 + col - 6
                else:
                    place = (432 if row >= 3 else 504) + level * 18 + (row % 3) * 6 + col
                natural_to_quad[source] = place
                quad_to_natural[place] = source
    index = 0
    for lev_win in range(2):
        for lon_win in range(2):
            for s in range(12):
                for p in range(2):
                    for r in range(6):
                        level = (lev_win * 2 + p + 1) % 4
                        col = lon_win * 12 + s
                        if col < 18:
                            place = (0 if r < 3 else 216) + level * 54 + (r % 3) * 18 + col
                        else:
                            place = (432 if r < 3 else 504) + level * 18 + (r % 3) * 6 + col - 18
                        window_to_quad[index] = place
                        quad_to_window[place] = index
                        index += 1
    cell_lane = np.full(640, -1, np.int32)
    bias_row = np.full(640, -1, np.int32)
    merged_token = np.full((2, 640), -1, np.int32)
    for lane in range(256):
        if lane % 16 < 12:
            cell_lane[lane] = (12 * (lane // 16) + 3 + lane % 16) % 192
    for k in range(WIN):
        s, p, r = k // 12, (k // 6) % 2, k % 6
        bias_row[k] = p * 256 + r * 23 + 11 - s
    for lon_win in range(2):
        for row in range(384):
            p, r, y, m = row // 192, (row // 32) % 6, (row // 16) % 2, row % 16
            if 0 <= m - lon_win * 6 < 6:
                merged_token[lon_win, row] = (2 * (m - lon_win * 6) + y) * 12 + p * 6 + r
    rows = [natural_to_quad, quad_to_natural, quad_to_window, window_to_quad]
    return np.stack(rows + [cell_lane, bias_row, merged_token[0], merged_token[1]])


def dot_nn(a, b):
    return lax.dot_general(a, b, (((1,), (0,)), ((), ())), preferred_element_type=F32)


def dot_nt(a, b):
    return lax.dot_general(a, b, (((1,), (1,)), ((), ())), preferred_element_type=F32)


def dot_tn(a, b):
    return lax.dot_general(a, b, (((0,), (0,)), ((), ())), preferred_element_type=F32)


def one_hot(rows, targets):
    ids = lax.broadcasted_iota(I32, (rows, targets.shape[1]), 0)
    return jnp.where(ids == targets, 1.0, 0.0).astype(BF16)


def statistics(values):
    centred = values - jnp.mean(values, axis=-1, keepdims=True)
    inverse = lax.rsqrt(jnp.mean(centred * centred, axis=-1, keepdims=True) + EPS)
    return centred * inverse, inverse


def norm_back(normed, inverse, scaled):
    centre = jnp.mean(scaled, axis=-1, keepdims=True)
    projected = jnp.mean(scaled * normed, axis=-1, keepdims=True)
    return inverse * (scaled - centre - normed * projected)


def gelu_parts(values):
    cumulative = 0.5 * (1.0 + lax.erf(values * (1.0 / math.sqrt(2.0))))
    density = jnp.exp(-0.5 * values * values) * (1.0 / math.sqrt(2.0 * math.pi))
    return values * cumulative, cumulative + values * density


def lanes(rows, cols):
    return lax.broadcasted_iota(I32, (rows, cols), 1)


def over_12(ids):
    return (ids * 5462) >> 16


def over_6(ids):
    return (ids * 10923) >> 16


def kernel(
    fields, cot, attend_gain, triple_w, bias, output_w, feed_gain, expand_w, shrink_t, merge_gain,
    merge_wt, orders,
    out_fields, out_g1, out_g2,
    sq, gq, a10, a01, a11, b10, b01, b11, c10, c01, c11, d10, d01, d11, x_w, ni_s, q_s, k_s, v_s, wq, wk, wv, p_s, att_s, mid_s, nm_s, act_s, slope_s, vo_s,
    b16, bl_s, bs_s, bx, ds_s, spread_s, pick_s,
    cells, cs, cx, cm, ch, planes, w_own, w_part, w_send, w_all, qry, qw, st, sx, sup, sdn, tup, tdn, cp_s, go_s, gh_s, gm_s, ga_s, gmh_s,
    dt_s, gt_s, raw, dsh, dam, hid, tmp, g1s, g1p, g1h, g1r, g1l, g1f, g1o, g2s, g2p, g2h, g2r, g2l, g2f, g2o,
    halo_ss, halo_rs, back_ss, back_rs, st_ss, st_rs, sends, recvs,
):
    e = lax.axis_index("lon")
    d = lax.axis_index("lat")
    e_up, e_dn = lax.rem(e + 1, NLON), lax.rem(e + NLON - 1, NLON)
    d_up, d_dn = lax.rem(d + 1, NLAT), lax.rem(d + NLAT - 1, NLAT)

    def remote(src, dst, ssem, rsem, device):
        return pltpu.make_async_remote_copy(
            src_ref=src, dst_ref=dst, send_sem=ssem, recv_sem=rsem, device_id=device,
            device_id_type=MESH,
        )

    core, chip = lax.rem(e, 2), e // 2
    partner = e + 1 - 2 * core
    d_pair = d + 1 - 2 * lax.rem(d, 2)

    def chips_all(action):
        def body(step, carry):
            action(lax.rem(chip + step, NCHIP))
            return carry

        lax.fori_loop(1, NCHIP, body, 0)

    def lat_all(action):
        def body(step, carry):
            action(lax.rem(d + step, NLAT))
            return carry

        lax.fori_loop(1, NLAT, body, 0)

    def to_chip(src, dst, phase, o):
        return remote(src, dst, sends.at[phase], recvs.at[phase], (2 * o + core, d))

    def to_band(src, dst, phase, o):
        return remote(src, dst, sends.at[phase], recvs.at[phase], (e, o))

    def to_core(src, dst, phase):
        return remote(src, dst, sends.at[phase], recvs.at[phase], (partner, d))

    def arrived(region, phase):
        remote(region, region, sends.at[phase], recvs.at[phase], (partner, d)).wait_recv()

    def left(region, phase):
        remote(region, region, sends.at[phase], recvs.at[phase], (partner, d)).wait_send()

    barrier = pltpu.get_barrier_semaphore()

    def greet(device):
        pl.semaphore_signal(barrier, inc=1, device_id=device, device_id_type=MESH)

    chips_all(lambda o: greet((2 * o + core, d)))
    lat_all(lambda o: greet((e, o)))
    for device in ((e_up, d), (e_dn, d), (e_up, d_up), (e_dn, d_dn)):
        greet(device)

    def half_rows(b):
        return pl.ds(pl.multiple_of(b * HALF, HALF), HALF)

    def pack(quads, b, out):
        at = 216
        for (size, cut), message in zip(SIZES, out):
            rows = quads[at:at + size]
            rest = jnp.concatenate([rows[cut:, 128:C], jnp.zeros((2 * cut - size, 64), F32)], axis=0)
            parts = [rows[:, 0:128], jnp.concatenate([rows[:cut, 128:C], rest], axis=1)]
            if (size + cut) % 16:
                parts.append(jnp.zeros((8, 128), F32))
            message[b] = jnp.concatenate(parts, axis=0).astype(BF16)
            at += size

    def unpack(quads, b, messages):
        at = 216
        for (size, cut), message in zip(SIZES, messages):
            rows = message[b].astype(F32)
            tails = rows[size:size + cut]
            tail = jnp.concatenate([tails[:, 0:64], tails[0:size - cut, 64:128]], axis=0)
            quads[b, at:at + size, :] = jnp.concatenate([rows[0:size], tail], axis=1)
            at += size

    def halo(sources, targets, ssem, rsem, step, b):
        devices = ((e, step[1]), (step[0], d), (step[0], step[1]))
        return [
            remote(src.at[b], dst.at[b], ssem.at[3 * b + i], rsem.at[3 * b + i], dev)
            for i, (src, dst, dev) in enumerate(zip(sources, targets, devices))
        ]

    def rows_ahead(b):
        return halo((a10, a01, a11), (b10, b01, b11), halo_ss, halo_rs, (e_dn, d_dn), b)

    def rows_behind(b):
        return halo((c10, c01, c11), (d10, d01, d11), back_ss, back_rs, (e_up, d_up), b)

    to_quad = one_hot(HALF, orders[0:1, 0:HALF])

    def sort_sample(b, carry):
        quads = dot_nn(to_quad, fields[half_rows(b), :])
        sq[b] = quads
        pack(quads, b, (a10, a01, a11))
        return carry

    lax.fori_loop(0, 2, sort_sample, 0)
    pl.semaphore_wait(barrier, NCHIP - 1 + NLAT - 1 + 4)
    for b in range(2):
        for copy in rows_ahead(b):
            copy.start()

    cells[...] = dot_nn(cot[...], one_hot(192, orders[4:5, 0:256]))
    block_of = lanes(72, 128) >> 4

    def gather_cells(inner, carry):
        for tile in range(2):
            piece = jnp.zeros((72, 128), F32)
            for bl in range(8):
                part = cells[bl * 72:(bl + 1) * 72, tile * 128:(tile + 1) * 128]
                part = pltpu.roll(part, lax.rem(16 * (bl - inner) + 128, 128), 1)
                piece = jnp.where(block_of == bl, part, piece)
            for a in range(3):
                padded = jnp.concatenate([piece[a * 24:(a + 1) * 24], jnp.zeros((8, 128), F32)], axis=0)
                cs[4 * tile + inner // 2, lax.rem(inner, 2), a] = padded.astype(BF16)
        return carry

    lax.fori_loop(0, 8, gather_cells, 0)
    w_own[...] = jnp.concatenate(
        [merge_wt[...].astype(F32), jnp.zeros((8, 768), F32)], axis=0
    ).astype(BF16)
    to_core(cs.at[:, 1 - core], cx, 0).start()
    to_core(w_own, w_part, 2).start()

    for h in range(HEADS):
        b16[2 * h:2 * h + 2, :] = bias[h]
    b16[12:16, :] = jnp.zeros((4, POS), F32)
    zero_tail = jnp.zeros((16, 256 - 138), F32)
    for p in range(2):
        for r in range(6):
            parts = []
            for pk in range(2):
                at = (p * 2 + pk) * 828 + r * 138
                parts += [b16[:, at:at + 138], zero_tail]
            row = jnp.concatenate(parts, axis=1)
            high = row.astype(BF16)
            low = (row - high.astype(F32)).astype(BF16)
            at = (p * 6 + r) * 16
            bl_s[at:at + 16, :] = high
            bl_s[192 + at:192 + at + 16, :] = low

    bias_row = orders[5:6, 0:WIN]

    def spread(pair, carry):
        for i in range(2):
            s_i = 2 * pair + i
            matrix = one_hot(512, bias_row + s_i)
            spread_s[s_i] = matrix
            split = dot_nn(bl_s[...], matrix)
            rows = split[0:192] + split[192:384]
            at = pl.ds(pl.multiple_of(s_i * 192, 192), 192)
            bs_s[0, at, :] = rows[:, 0:128]
            bs_s[1, at, :] = jnp.concatenate([rows[:, 128:144], jnp.zeros((192, 112), F32)], axis=1)
        return carry

    lax.fori_loop(0, 6, spread, 0)

    def dense(mine, other):
        mine, other = mine.astype(F32)[0:24], other.astype(F32)[0:24]
        swapped = core == 1
        parts = [jnp.where(swapped, other, mine), jnp.where(swapped, mine, other)]
        return jnp.concatenate(parts, axis=0)

    def chip_rows(o):
        return pl.ds(pl.multiple_of(o * 48, 48), 48)

    def merge_pieces(o, carry):
        for a in range(3):
            cm[o, a] = dense(cs[o, core, a], cx[o, a]).astype(BF16)
        return carry

    arrived(cx, 0)
    lax.fori_loop(0, NCHIP, merge_pieces, 0)
    planes[:, chip_rows(chip)] = cm[chip]
    chips_all(lambda o: to_chip(cm.at[o], planes.at[:, chip_rows(chip)], 1, o).start())
    arrived(w_part, 2)
    both = dense(w_own[...], w_part[...])
    w_send[...] = jnp.where(core == 1, both[:, 384:768], both[:, 0:384]).astype(BF16)
    w_all[core, chip_rows(chip)] = w_send[...]
    chips_all(lambda o: to_chip(w_send, w_all.at[core, chip_rows(chip)], 3, o).start())
    seven = pl.ds(0, 48 * (NCHIP - 1))

    tok_i = lax.broadcasted_iota(I32, (WIN, WIN), 0)
    tok_k = lax.broadcasted_iota(I32, (WIN, WIN), 1)
    half_i, half_k = over_6(tok_i), over_6(tok_k)
    last_band = d == NLAT - 1
    lat_differs = ((tok_i - half_i * 6 >= 3) != (tok_k - half_k * 6 >= 3)) & last_band
    lev_differs = (half_i & 1) != (half_k & 1)
    bx[:, :, HEADS * WIN:WIDE] = jnp.zeros((2, WIN, WIDE - HEADS * WIN), F32)
    for lw in range(2):
        differs = (lat_differs | lev_differs) if lw else lat_differs
        for h in range(HEADS):
            at = pl.ds(h * 2 + lw, WIN, stride=16)
            full = jnp.concatenate([bs_s.at[0][at, :], bs_s.at[1][at, :]], axis=1)[:, 0:WIN]
            spread_bias = jnp.where(differs, MASKED, full).T
            bx[lw, :, h * 128:(h + 1) * 128] = spread_bias[:, 0:128]
            bx[lw, :, 768 + h * 16:784 + h * 16] = spread_bias[:, 128:WIN]

    wq[...] = triple_w[:, 0:192]
    wk[...] = triple_w[:, 192:384]
    wv[...] = triple_w[:, 384:576]

    head_of = lanes(1, C) >> 5
    head_f = [jnp.where(head_of == h, 1.0, 0.0) for h in range(HEADS)]
    head_b = [mask.astype(BF16) for mask in head_f]

    blank = jnp.zeros((WIDE - HEADS * WIN, C), BF16)

    def stacked(values):
        first, rest = values[0:128], values[128:WIN]
        parts = [first * mask for mask in head_b] + [rest * mask for mask in head_b]
        return jnp.concatenate(parts + [blank], axis=0)

    def per_head(left, right):
        turned = left.T
        wide = [dot_nn(turned[64 * i:64 * i + 64], right[:, 256 * i:256 * i + 256]) for i in range(3)]
        tail = dot_nn(turned, right[:, 768:WIDE])
        blocks = []
        for h in range(HEADS):
            at, row = 128 * (h % 2), 32 * (h % 2)
            blocks.append(
                jnp.concatenate(
                    [wide[h // 2][row:row + 32, at:at + 128], tail[32 * h:32 * h + 32, 16 * h:16 * h + 16]], axis=1
                )
            )
        return jnp.concatenate(blocks, axis=0).T

    to_window = one_hot(HALF, orders[2:3, 0:HALF])

    def window_rows(w):
        return pl.ds(pl.multiple_of(w * WIN, WIN), WIN)

    def chunk_rows(i):
        return pl.ds(pl.multiple_of(i * CHUNK, CHUNK), CHUNK)

    def tile_rows(i, t):
        return pl.ds(pl.multiple_of(i * CHUNK + t * TILE, 16), TILE)

    def project(i, carry):
        rows = chunk_rows(i)
        for t in range(CHUNK // TILE):
            part = tile_rows(i, t)
            normed = statistics(x_w[part, :].astype(F32))[0]
            ni_s[part, :] = (normed * attend_gain[...]).astype(BF16)
        normed_in = ni_s[rows, :]
        q_s[rows, :] = dot_nn(normed_in, wq[...]).astype(BF16)
        k_s[rows, :] = dot_nn(normed_in, wk[...]).astype(BF16)
        v_s[rows, :] = dot_nn(normed_in, wv[...]).astype(BF16)
        return carry


    def attend(pair, carry):
        lw = lax.rem(pair, 2)
        for i in range(2):
            rows = window_rows(2 * pair + i)
            raw[i] = dot_nt(k_s[rows, :], stacked(q_s[rows, :]))
        for i in range(2):
            for t in range(WIDE // 128):
                cols = slice(t * 128, (t + 1) * 128)
                scores = raw[i, :, cols] * FACTOR + bx[lw, :, cols]
                exponent = jnp.exp(scores - jnp.max(scores, axis=0, keepdims=True))
                chances = exponent * (1.0 / jnp.sum(exponent, axis=0, keepdims=True))
                p_s[2 * pair + i, :, cols] = chances.astype(BF16)
        for i in range(2):
            rows = window_rows(2 * pair + i)
            att_s[rows, :] = per_head(v_s[rows, :], p_s[2 * pair + i]).astype(BF16)
        return carry

    def forward_windows(b, carry):
        for copy in rows_ahead(b):
            copy.wait()

        unpack(sq, b, (b10, b01, b11))
        x_w[half_rows(b), :] = dot_nn(to_window, sq[b].astype(BF16)).astype(BF16)
        lax.fori_loop(2 * b, 2 * b + 2, project, 0)

        lax.fori_loop(2 * b, 2 * b + 2, attend, 0)

        @pl.when(b == 0)
        def _():
            arrived(planes.at[:, seven], 1)
            to_band(planes.at[pl.ds(0, 2)], ch, 4, d_dn).start()

        return carry

    lax.fori_loop(0, 2, forward_windows, 0)
    arrived(w_all.at[0, seven], 3)
    to_core(w_all.at[core], w_all.at[core], 16).start()

    def feed(i, carry):
        rows = chunk_rows(i)
        tmp[...] = x_w[rows, :].astype(F32) + dot_nn(att_s[rows, :], output_w[...])
        for t in range(CHUNK // TILE):
            part = tile_rows(i, t)
            middle = tmp[t * TILE:(t + 1) * TILE, :]
            mid_s[part, :] = middle
            nm_s[part, :] = (statistics(middle)[0] * feed_gain[...]).astype(BF16)
        hid[...] = dot_nn(nm_s[rows, :], expand_w[...])
        for t in range(CHUNK // 16):
            part = pl.ds(pl.multiple_of(i * CHUNK + t * 16, 16), 16)
            for j in range(FF // 256):
                cols = slice(j * 256, (j + 1) * 256)
                act, slope = gelu_parts(hid[t * 16:(t + 1) * 16, cols])
                act_s[part, cols] = act.astype(BF16)
                slope_s[part, cols] = slope
        vo_s[rows, :] = (tmp[...] + dot_nt(act_s[rows, :], shrink_t[...])).astype(BF16)
        return carry

    lax.fori_loop(0, NCHUNK, feed, 0)

    arrived(w_all.at[0], 16)
    gain_row = merge_gain[...].reshape(1, 4 * C)
    for r in range(6):
        x = (r + 1) % 2
        cell = (0, 1, 1, 2, 2, 3)[r]
        cols = slice(x * 384, (x + 1) * 384)
        if r == 3:
            arrived(ch, 4)
        plane = planes[cell + 1] if cell < 2 else ch[cell - 2]
        summed = dot_tn(plane, w_all[x])
        scaled = summed * gain_row[:, x * 384:(x + 1) * 384]
        qry[2 * r] = scaled[:, 0:192].astype(BF16)
        qry[2 * r + 1] = scaled[:, 192:384].astype(BF16)

    st[...] = jnp.zeros_like(st)
    for i in range(2):
        pick_s[i] = one_hot(WIN, orders[6 + i:7 + i, 0:384])
    stat_lane = lanes(WIN, 128)
    tile_lane = lanes(TILE, 128)

    def merge_sums(w, carry):
        rows = window_rows(w)
        b, lw, lon_win = w // 4, lax.rem(w // 2, 2), lax.rem(w, 2)
        parts = []
        for p in range(2):
            level = lax.rem(lw * 2 + p + 1, 4)
            at = pl.ds(pl.multiple_of((b * 4 + level) * 16, 16), 16)
            parts.append(qry[:, at, :].reshape(192, C))
        qw[rows, :] = dot_nn(pick_s[lon_win], jnp.concatenate(parts, axis=0)).astype(BF16)
        for t in range(WIN // TILE):
            part = pl.ds(pl.multiple_of(w * WIN + t * TILE, 16), TILE)
            at = slice(t * TILE, (t + 1) * TILE)
            q = qw[part, :].astype(F32)
            v = vo_s[part, :].astype(F32)
            mean = jnp.mean(v, axis=-1, keepdims=True)
            centred = v - mean
            squares = jnp.sum(centred * centred, axis=-1, keepdims=True)
            q_sum = jnp.sum(q, axis=-1, keepdims=True)
            qv_sum = jnp.sum(q * centred, axis=-1, keepdims=True)
            total = st[b, at, :]
            for j, value in enumerate((mean, squares, q_sum, qv_sum)):
                total = jnp.where(tile_lane == 32 * j + w, value, total)
            st[b, at, :] = total
        return carry

    def sums_copies(b):
        return (
            remote(tup.at[b], sup.at[b], st_ss.at[2 * b], st_rs.at[2 * b], (e, d_up)),
            remote(tdn.at[b], sdn.at[b], st_ss.at[2 * b + 1], st_rs.at[2 * b + 1], (e, d_dn)),
        )

    def exchange(b):
        tup[b] = st.at[b][pl.ds(5, 24, stride=6), :]
        tdn[b] = st.at[b][pl.ds(0, 24, stride=6), :]
        for copy in sums_copies(b):
            copy.start()

    even = (over_12(lax.broadcasted_iota(I32, (WIN, 128), 0)) & 1) == 0

    def pair_of(values):
        return jnp.where(even, pltpu.roll(values, WIN - 12, 0), pltpu.roll(values, 12, 0))

    def cell_norm(b):
        for r, other in ((1, 2), (2, 1), (3, 4), (4, 3)):
            sx[pl.ds(r, 24, stride=6), :] = st.at[b][pl.ds(other, 24, stride=6), :]
        for copy in sums_copies(b):
            copy.wait()
        sx[pl.ds(0, 24, stride=6), :] = sup[b]
        sx[pl.ds(5, 24, stride=6), :] = sdn[b]
        own, cross = st[b], sx[...]
        group = [own, cross, pair_of(own), pair_of(cross)]
        cell_mean = (group[0] + group[1] + group[2] + group[3]) * 0.25
        variance = jnp.zeros((WIN, 128), F32)
        q_total = jnp.zeros((WIN, 128), F32)
        qv_total = jnp.zeros((WIN, 128), F32)
        for values in group:
            offset = values - cell_mean
            q_sum = pltpu.roll(values, 64, 1)
            variance = variance + pltpu.roll(values, 96, 1) + 192.0 * offset * offset
            q_total = q_total + q_sum
            qv_total = qv_total + pltpu.roll(values, 32, 1) + offset * q_sum
        cell_inverse = lax.rsqrt(jnp.where(stat_lane < 8, variance, 0.0) * (1.0 / 768.0) + EPS)
        cp_s[0] = cell_mean
        cp_s[1] = cell_inverse
        cp_s[2] = q_total * (1.0 / 768.0)
        cp_s[3] = cell_inverse * cell_inverse * qv_total * (1.0 / 768.0)

    def merge_back(w, carry):
        for t in range(WIN // TILE):
            part = pl.ds(pl.multiple_of(w * WIN + t * TILE, 16), TILE)
            at = slice(t * TILE, (t + 1) * TILE)
            mean, inverse, q_mean, projected = [
                jnp.sum(jnp.where(tile_lane == w, cp_s[j, at, :], 0.0), axis=-1, keepdims=True) for j in range(4)
            ]
            v = vo_s[part, :].astype(F32) - mean
            go_s[part, :] = (inverse * (qw[part, :].astype(F32) - q_mean - v * projected)).astype(BF16)
        return carry

    def feed_back(i, carry):
        rows = chunk_rows(i)
        go = go_s[rows, :]
        gh = (dot_nn(go, shrink_t[...]) * slope_s[rows, :]).astype(BF16)
        gh_s[rows, :] = gh
        tmp[...] = dot_nt(gh, expand_w[...])
        for t in range(CHUNK // TILE):
            part = tile_rows(i, t)
            gnm = tmp[t * TILE:(t + 1) * TILE, :]
            unit, inverse = statistics(mid_s[part, :])
            gm = go_s[part, :].astype(F32) + norm_back(unit, inverse, gnm * feed_gain[...])
            gm_s[part, :] = gm
            gmh_s[part, :] = gm.astype(BF16)
        ga_s[rows, :] = dot_nt(gmh_s[rows, :], output_w[...]).astype(BF16)
        return carry

    def forward_sample(b, carry):
        lax.fori_loop(4 * b, 4 * b + 4, merge_sums, 0)
        exchange(b)
        return carry

    def backward_sample(b, carry):
        cell_norm(b)
        lax.fori_loop(4 * b, 4 * b + 4, merge_back, 0)
        lax.fori_loop(2 * b, 2 * b + 2, feed_back, 0)
        return carry

    lax.fori_loop(0, 2, forward_sample, 0)
    ds_s[...] = jnp.zeros_like(ds_s)
    dt_s[...] = jnp.zeros_like(dt_s)
    from_window = one_hot(HALF, orders[3:4, 0:HALF])
    lax.fori_loop(0, 2, backward_sample, 0)

    g_expand = dot_tn(nm_s[...], gh_s[...]).astype(BF16)
    g_shrink = dot_tn(go_s[...], act_s[...]).astype(BF16)
    g_output = dot_tn(att_s[...], gmh_s[...]).astype(BF16)
    for i in range(4):
        for j in range(2):
            g1s[0, 2 * i + j, 0:48] = g_expand[i * 48:(i + 1) * 48, j * 384:(j + 1) * 384]
            g1s[1, 2 * i + j, 0:48] = g_shrink[i * 48:(i + 1) * 48, j * 384:(j + 1) * 384]
    wide = jnp.concatenate([g_output[0:96], g_output[96:192]], axis=1)
    for i in range(NCHIP):
        for j in range(2):
            at = (i * 2 + j) * 16
            g1s[j, i, 48:64] = wide[at:at + 16] if at < 96 else jnp.zeros((16, 384), BF16)

    def sum_of(ref, count, rows):
        total = ref[0, rows].astype(F32)
        for o in range(1, count):
            total = total + ref[o, rows].astype(F32)
        return total.astype(BF16)

    def add_pair(mine, other, out):
        def body(o, carry):
            out[o] = (mine[core, o].astype(F32) + other[o].astype(F32)).astype(BF16)
            return carry

        lax.fori_loop(0, NCHIP, body, 0)

    others = pl.ds(0, NCHIP - 1)
    to_core(g1s.at[1 - core], g1p, 5).start()


    def attend_back(pair, carry):
        lw = lax.rem(pair, 2)
        for i in range(2):
            rows = window_rows(2 * pair + i)
            dam[i] = stacked(ga_s[rows, :])
            raw[i] = dot_nt(v_s[rows, :], dam[i])
        for i in range(2):
            for t in range(WIDE // 128):
                cols = slice(t * 128, (t + 1) * 128)
                chances = p_s[2 * pair + i, :, cols].astype(F32)
                weighted = raw[i, :, cols]
                centre = jnp.sum(chances * weighted, axis=0, keepdims=True)
                dsh[i, :, cols] = (chances * (weighted - centre)).astype(BF16)
        for i in range(2):
            rows = window_rows(2 * pair + i)
            dt_s[rows, 512:704] = dot_nn(p_s[2 * pair + i], dam[i]).astype(BF16)
            dt_s[rows, 0:C] = (per_head(k_s[rows, :], dsh[i]) * FACTOR).astype(BF16)
            dt_s[rows, 256:448] = (dot_nn(dsh[i], stacked(q_s[rows, :])) * FACTOR).astype(BF16)
        ds_s[lw] = ds_s[lw] + (dsh[0].astype(F32) + dsh[1].astype(F32))
        return carry

    all_rows = slice(0, 64)
    def windows_back(pair, carry):
        attend_back(pair, carry)

        @pl.when(pair == 0)
        def _():
            arrived(g1p, 5)
            add_pair(g1s, g1p, g1h)
            g1r[chip] = g1h[chip]
            chips_all(lambda o: to_chip(g1h.at[o], g1r.at[chip], 6, o).start())

        @pl.when(pair == 2)
        def _():
            arrived(g1l.at[pl.ds(0, 3)], 7)
            g1l[4] = sum_of(g1l, 4, all_rows)
            to_band(g1l.at[4], g1l.at[5], 15, d_pair).start()

        return carry

    def second_gradients():
        summed = dot_tn(ni_s[...], dt_s[...])
        sections = [summed[:, 0:C], summed[:, 256:448], summed[:, 512:704], jnp.zeros((C, 64), F32)]
        g_triple = jnp.concatenate(sections, axis=1).astype(BF16)
        for i in range(3):
            for j in range(5):
                at = 5 * i + j
                g2s[at // 8, at % 8, 0:64] = g_triple[i * 64:(i + 1) * 64, j * 128:(j + 1) * 128]
        g2s[1, 7, 0:64] = jnp.zeros((64, 128), BF16)
        arrived(g1l.at[5], 15)
        g1f[chip] = (g1l[4].astype(F32) + g1l[5].astype(F32)).astype(BF16)
        chips_all(lambda o: to_chip(g1f.at[chip], g1f.at[chip], 8, o).start())
        for lw in range(2):
            for h in range(HEADS):
                at = pl.ds(h * 2 + lw, WIN, stride=16)
                part = jnp.concatenate(
                [ds_s[lw, :, h * 128:(h + 1) * 128], ds_s[lw, :, 768 + h * 16:784 + h * 16]], axis=1
            ).T
                bs_s.at[0][at, :] = part[:, 0:128]
                bs_s.at[1][at, :] = jnp.concatenate([part[:, 128:144], jnp.zeros((WIN, 112), F32)], axis=1)

        def fold(s_i):
            at = slice(s_i * 192, (s_i + 1) * 192)
            rows = jnp.concatenate([bs_s[0, at, :], bs_s[1, at, :]], axis=1)[:, 0:WIN].astype(BF16)
            return dot_nt(rows, spread_s[s_i])

        folded = fold(0)
        for s_i in range(1, 12):
            folded = folded + fold(s_i)
        pieces_t = []
        for p in range(2):
            for pk in range(2):
                for r in range(6):
                    at = (p * 6 + r) * 16
                    pieces_t.append(folded[at:at + 16, pk * 256:pk * 256 + 138])
        table = jnp.concatenate(pieces_t + [jnp.zeros((16, 4096 - POS), F32)], axis=1).astype(BF16)
        for o in range(32):
            g2s[o // 16, (o // 2) % 8, 64 + 16 * (o % 2):80 + 16 * (o % 2)] = table[:, o * 128:(o + 1) * 128]
        to_core(g2s.at[1 - core], g2p, 9).start()

    def project_back(i, carry):
        rows = chunk_rows(i)
        tmp[...] = (
            dot_nt(dt_s[rows, 0:C], wq[...])
            + dot_nt(dt_s[rows, 256:448], wk[...])
            + dot_nt(dt_s[rows, 512:704], wv[...])
        )
        for t in range(CHUNK // TILE):
            part = tile_rows(i, t)
            unit, inverse = statistics(x_w[part, :].astype(F32))
            back = norm_back(unit, inverse, tmp[t * TILE:(t + 1) * TILE, :] * attend_gain[...])
            gt_s[part, :] = (gm_s[part, :] + back).astype(BF16)
        return carry

    def backward_windows(b, carry):
        lax.fori_loop(2 * b, 2 * b + 2, windows_back, 0)

        @pl.when(b == 1)
        def _():
            second_gradients()

        lax.fori_loop(2 * b, 2 * b + 2, project_back, 0)

        @pl.when(b == 1)
        def _():
            arrived(g2p, 9)
            add_pair(g2s, g2p, g2h)
            g2r[chip] = g2h[chip]
            chips_all(lambda o: to_chip(g2h.at[o], g2r.at[chip], 10, o).start())

        quads = dot_nn(from_window, gt_s[half_rows(b), :])
        gq[b] = quads
        pack(quads, b, (c10, c01, c11))
        for copy in rows_behind(b):
            copy.start()

        @pl.when(b == 0)
        def _():
            arrived(g1r.at[others], 6)
            g1l[d // 2] = sum_of(g1r, NCHIP, all_rows)
            for step in range(1, 4):
                to_band(g1l.at[d // 2], g1l.at[d // 2], 7, lax.rem(d + 2 * step, NLAT)).start()

        return carry

    lax.fori_loop(0, 2, backward_windows, 0)

    arrived(g1f.at[others], 8)
    to_core(g1f, g1o, 11).start()

    arrived(g2r.at[others], 10)
    g2l[d] = sum_of(g2r, NCHIP, slice(0, 64))
    lat_all(lambda o: to_band(g2l.at[d], g2l.at[d], 12, o).start())
    g2f[chip, 64:96] = sum_of(g2r, NCHIP, slice(64, 96))

    to_natural = one_hot(HALF, orders[1:2, 0:HALF])

    def unsort_sample(b, carry):
        for copy in rows_behind(b):
            copy.wait()
        unpack(gq, b, (d10, d01, d11))
        out_fields[half_rows(b), :] = dot_nn(to_natural, gq[b].astype(BF16)).astype(BF16)
        return carry

    lax.fori_loop(0, 1, unsort_sample, 0)
    arrived(g2l.at[others], 12)
    g2f[chip, 0:64] = sum_of(g2l, NLAT, slice(0, 64))
    chips_all(lambda o: to_chip(g2f.at[chip], g2f.at[chip], 13, o).start())


    lax.fori_loop(1, 2, unsort_sample, 0)
    arrived(g1o, 11)
    out_g1[core] = g1f[...]
    out_g1[1 - core] = g1o[...]
    arrived(g2f.at[others], 13)
    to_core(g2f, g2o, 14).start()
    out_g2[core] = g2f[...]
    arrived(g2o, 14)
    out_g2[1 - core] = g2o[...]

    left(cx, 0)
    left(cm.at[others], 1)
    left(w_part, 2)
    left(w_all.at[0, seven], 3)
    left(w_all.at[0], 16)
    left(ch, 4)
    left(g1p, 5)
    left(g1r.at[others], 6)
    left(g1l.at[pl.ds(0, 3)], 7)
    left(g1l.at[4], 15)
    left(g1f.at[others], 8)
    left(g2p, 9)
    left(g2r.at[others], 10)
    left(g1o, 11)
    left(g2l.at[others], 12)
    left(g2f.at[others], 13)
    left(g2o, 14)


def results_kernel(
    fields, g1, g2, attend_gain, triple_w, feed_gain, expand_w,
    out_fields, out_triple, out_output, out_expand, out_shrink, out_attend, out_feed, out_table,
):
    out_fields[...] = fields[...]
    for i in range(4):
        for j in range(2):
            rows, cols = slice(i * 48, (i + 1) * 48), slice(j * 384, (j + 1) * 384)
            out_expand[rows, cols] = g1[0, 2 * i + j, 0:48].astype(F32)
            out_shrink[rows, cols] = g1[1, 2 * i + j, 0:48].astype(F32)
    for i in range(6):
        wide = g1[i % 2, i // 2, 48:64].astype(F32)
        out_output[i * 16:(i + 1) * 16, :] = wide[:, 0:C]
        out_output[96 + i * 16:96 + (i + 1) * 16, :] = wide[:, C:2 * C]
    for i in range(3):
        for j in range(5):
            at, size = 5 * i + j, 128 if j < 4 else 64
            part = g2[at // 8, at % 8, 0:64].astype(F32)
            out_triple[i * 64:(i + 1) * 64, j * 128:j * 128 + size] = part[:, 0:size]
    table = jnp.concatenate(
        [g2[o // 16, (o // 2) % 8, 64 + 16 * (o % 2):80 + 16 * (o % 2)] for o in range(32)], axis=1
    ).astype(F32)
    for h in range(HEADS):
        out_table[h] = table[2 * h:2 * h + 2, 0:POS]

    def gain_gradient(grad, weight, gain):
        product = (grad[...] * weight[...].astype(F32)).astype(BF16)
        total = dot_nt(jnp.ones((16, product.shape[1]), BF16), product)
        return total[0:1] / gain[...]

    out_attend[...] = gain_gradient(out_triple, triple_w, attend_gain)
    out_feed[...] = gain_gradient(out_expand, expand_w, feed_gain)


def scratch():
    def vmem(*shape, kind=BF16):
        return pltpu.VMEM(shape, kind)

    token = vmem(TOK, C)
    token_f = vmem(TOK, C, kind=F32)
    weight = vmem(C, C)
    quad = vmem(2, HALF, C, kind=F32)
    halves = [vmem(2, 336, 128), vmem(2, 112, 128), vmem(2, 112, 128)]
    stat = vmem(WIN, 128, kind=F32)
    small = vmem(2, 24, 128, kind=F32)
    buffers = [
        quad, quad, *halves, *halves, *halves, *halves, token, token, token, token, token, weight, weight, weight,
        vmem(NWIN, WIN, WIDE), token, token_f, token, vmem(TOK, FF), vmem(TOK, FF, kind=F32), token,
        vmem(16, POS, kind=F32), vmem(384, 512), vmem(2, 2304, 128, kind=F32),
        vmem(2, WIN, WIDE, kind=F32), vmem(2, WIN, WIDE, kind=F32),
        vmem(12, 512, WIN), vmem(2, WIN, 384),
        vmem(576, 256, kind=F32), vmem(8, 2, 3, 32, 128), vmem(8, 3, 32, 128),
        vmem(8, 3, 48, 128), vmem(2, 384, 128), vmem(3, 384, 128),
        vmem(32, 768), vmem(32, 768), vmem(48, 384), vmem(2, 384, 384),
        vmem(12, 128, C), token, vmem(2, WIN, 128, kind=F32), stat, small, small, small, small, vmem(4, WIN, 128, kind=F32),
        token, vmem(TOK, FF), token_f, token, token, vmem(TOK, 768), token,
        vmem(2, WIN, WIDE, kind=F32), vmem(2, WIN, WIDE), vmem(2, WIDE, C), vmem(CHUNK, FF, kind=F32),
        vmem(CHUNK, C, kind=F32),
    ]
    for rows, cols in ((64, 384), (96, 128)):
        chunks = vmem(8, rows, cols)
        buffers += [vmem(2, 8, rows, cols), chunks, chunks, chunks, vmem(8, 64, cols), chunks, chunks]
    counts = [6, 6, 6, 6, 4, 4, 17, 17]
    return buffers + [pltpu.SemaphoreType.DMA((n,)) for n in counts]


def per_device(
    fields, merge_cotangent, attend_gain, triple_weight, bias_table, output_weight, feed_gain,
    expand_weight, shrink_weight, merge_gain, merge_weight,
):
    cot = jnp.transpose(merge_cotangent, (1, 2, 3, 4, 0)).reshape(576, 192)
    bias = jnp.transpose(bias_table[0], (1, 0, 2))
    def shaped(shapes):
        return [jax.ShapeDtypeStruct(shape, kind) for shape, kind in shapes]

    vmem_spec = pl.BlockSpec(memory_space=pltpu.VMEM)
    parts = pl.pallas_call(
        kernel,
        out_shape=shaped(
            [((TOK, C), BF16), ((2, 8, 64, 384), BF16), ((2, 8, 96, 128), BF16)]
        ),
        in_specs=[vmem_spec] * 12,
        out_specs=[vmem_spec] * 3,
        scratch_shapes=scratch(),
        compiler_params=pltpu.CompilerParams(
            collective_id=0, has_side_effects=True, vmem_limit_bytes=60 * 1024 * 1024
        ),
    )(
        fields.reshape(TOK, C), cot, attend_gain.reshape(1, C), triple_weight, bias, output_weight,
        feed_gain.reshape(1, C), expand_weight, shrink_weight.T, merge_gain,
        merge_weight.T, jnp.asarray(order_indices()),
    )
    g_fields, g_triple, g_output, g_expand, g_shrink, g_attend, g_feed, g_table = pl.pallas_call(
        results_kernel,
        out_shape=shaped(
            [
                ((TOK, C), BF16), ((C, 3 * C), F32), ((C, C), F32), ((C, FF), F32), ((C, FF), F32),
                ((1, C), F32), ((1, C), F32), ((HEADS, 2, POS), F32),
            ]
        ),
        in_specs=[vmem_spec] * 7,
        out_specs=[vmem_spec] * 8,
        compiler_params=pltpu.CompilerParams(vmem_limit_bytes=60 * 1024 * 1024),
    )(*parts, attend_gain.reshape(1, C), triple_weight, feed_gain.reshape(1, C), expand_weight)
    return (
        g_fields.reshape(fields.shape), g_triple, g_output, g_expand, g_shrink.T,
        g_attend.reshape(C), g_feed.reshape(C), jnp.transpose(g_table, (1, 0, 2))[None],
    )


def solution(mesh):
    placed = (
        P(None, None, "lat", "lon", None),
        P(None, None, None, "lat", "lon"),
        P(),
        P(),
        P("lat", None, None, None),
        P(),
        P(),
        P(),
        P(),
        P(),
        P(None, "lon"),
    )
    return jax.shard_map(
        per_device,
        mesh=mesh,
        in_specs=placed,
        out_specs=(
            P(None, None, "lat", "lon", None),
            P(),
            P(),
            P(),
            P(),
            P(),
            P(),
            P("lat", None, None, None),
        ),
        check_vma=False,
    )
```

profile of v0, /device:TPU:1, one launch (start us, length us, event | category | flops | bytes accessed | tf_op | source)
XLA Modules:
  0.0 89.8 jit_solution(4385362756929733596)
XLA Ops:
  0.6 86.0 %shard_map.179 = (bf16[1152,192]{1,0:T(8,128)(2,1)}, bf16[2,8,64,384]{3,2,1,0:T(8,128)(2,1)}, bf16[2,8,96,128]{3,2,1,0:T(8,128)(2,1)}) custom-call(bf16[1152,192]{1,0:T(8,128)(2,1)} %bitcast.18, bf16[576,192]{1,0:T(8,128)(2,1)} %bitcast.19, f32[1,192]{1,0:T(1,128)} %bitcast.23, bf16[192,576]{1,0:T(8,128)(2,1)} %triple_w.3, f32[6,2,3312]{2,1,0:T(2,128)} %bitcast.21, ...), custom_call_target="tpu_custom_call" | custom-call | tf_op jit(solution)/shard_map/pallas_call | solution.py:871
  86.6 3.2 %shard_map.180 = (bf16[1152,192]{1,0:T(8,128)(2,1)}, f32[192,576]{1,0:T(8,128)}, f32[192,192]{1,0:T(8,128)}, f32[192,768]{1,0:T(8,128)}, f32[192,768]{1,0:T(8,12...) custom-call(bf16[1152,192]{1,0:T(8,128)(2,1)} %get-tuple-element.19.fields, ...), custom_call_target="tpu_custom_call" | custom-call | tf_op jit(solution)/shard_map/pallas_call | solution.py:887
where the time goes:
time: 90 us; the launch traced here: 89.8 us
  Pallas kernels  89.2 us (99%)
    pallas_call x1, Pallas kernels, per_device(): pl.pallas_call(kernel, out_shape=shaped([((TOK, C), BF16), ((2, 8, 64, 38...  86 us
    pallas_call x1, Pallas kernels, per_device(): pl.pallas_call(results_kernel, out_shape=shaped([((TOK, C), BF16), ((C, 3...  3.2 us

commit v1 on v0

--- a/solution.py
+++ b/solution.py
@@ -28,7 +28,7 @@
 HALF = TOK // 2
 SIZES = ((216, 112), (72, 40), (72, 40))
 POS = 3312
-CHUNK = 288
+CHUNK = 576
 NCHUNK = TOK // CHUNK
 TILE = 48
 WIDE = 896
@@ -416,7 +416,7 @@
 
         unpack(sq, b, (b10, b01, b11))
         x_w[half_rows(b), :] = dot_nn(to_window, sq[b].astype(BF16)).astype(BF16)
-        lax.fori_loop(2 * b, 2 * b + 2, project, 0)
+        project(b, carry)
 
         lax.fori_loop(2 * b, 2 * b + 2, attend, 0)
 
@@ -472,28 +472,31 @@
     stat_lane = lanes(WIN, 128)
     tile_lane = lanes(TILE, 128)
 
-    def merge_sums(w, carry):
-        rows = window_rows(w)
-        b, lw, lon_win = w // 4, lax.rem(w // 2, 2), lax.rem(w, 2)
+    def merge_sums(pair, carry):
+        b, lw = pair // 2, lax.rem(pair, 2)
         parts = []
         for p in range(2):
             level = lax.rem(lw * 2 + p + 1, 4)
             at = pl.ds(pl.multiple_of((b * 4 + level) * 16, 16), 16)
             parts.append(qry[:, at, :].reshape(192, C))
-        qw[rows, :] = dot_nn(pick_s[lon_win], jnp.concatenate(parts, axis=0)).astype(BF16)
+        cells_q = jnp.concatenate(parts, axis=0)
+        for i in range(2):
+            qw[window_rows(2 * pair + i), :] = dot_nn(pick_s[i], cells_q).astype(BF16)
         for t in range(WIN // TILE):
-            part = pl.ds(pl.multiple_of(w * WIN + t * TILE, 16), TILE)
             at = slice(t * TILE, (t + 1) * TILE)
-            q = qw[part, :].astype(F32)
-            v = vo_s[part, :].astype(F32)
-            mean = jnp.mean(v, axis=-1, keepdims=True)
-            centred = v - mean
-            squares = jnp.sum(centred * centred, axis=-1, keepdims=True)
-            q_sum = jnp.sum(q, axis=-1, keepdims=True)
-            qv_sum = jnp.sum(q * centred, axis=-1, keepdims=True)
             total = st[b, at, :]
-            for j, value in enumerate((mean, squares, q_sum, qv_sum)):
-                total = jnp.where(tile_lane == 32 * j + w, value, total)
+            for i in range(2):
+                w = 2 * pair + i
+                part = pl.ds(pl.multiple_of(w * WIN + t * TILE, 16), TILE)
+                q = qw[part, :].astype(F32)
+                v = vo_s[part, :].astype(F32)
+                mean = jnp.mean(v, axis=-1, keepdims=True)
+                centred = v - mean
+                squares = jnp.sum(centred * centred, axis=-1, keepdims=True)
+                q_sum = jnp.sum(q, axis=-1, keepdims=True)
+                qv_sum = jnp.sum(q * centred, axis=-1, keepdims=True)
+                for j, value in enumerate((mean, squares, q_sum, qv_sum)):
+                    total = jnp.where(tile_lane == 32 * j + w, value, total)
             st[b, at, :] = total
         return carry
 
@@ -539,15 +542,17 @@
         cp_s[2] = q_total * (1.0 / 768.0)
         cp_s[3] = cell_inverse * cell_inverse * qv_total * (1.0 / 768.0)
 
-    def merge_back(w, carry):
-        for t in range(WIN // TILE):
-            part = pl.ds(pl.multiple_of(w * WIN + t * TILE, 16), TILE)
-            at = slice(t * TILE, (t + 1) * TILE)
-            mean, inverse, q_mean, projected = [
-                jnp.sum(jnp.where(tile_lane == w, cp_s[j, at, :], 0.0), axis=-1, keepdims=True) for j in range(4)
-            ]
-            v = vo_s[part, :].astype(F32) - mean
-            go_s[part, :] = (inverse * (qw[part, :].astype(F32) - q_mean - v * projected)).astype(BF16)
+    def merge_back(pair, carry):
+        for i in range(2):
+            w = 2 * pair + i
+            for t in range(WIN // TILE):
+                part = pl.ds(pl.multiple_of(w * WIN + t * TILE, 16), TILE)
+                at = slice(t * TILE, (t + 1) * TILE)
+                mean, inverse, q_mean, projected = [
+                    jnp.sum(jnp.where(tile_lane == w, cp_s[j, at, :], 0.0), axis=-1, keepdims=True) for j in range(4)
+                ]
+                v = vo_s[part, :].astype(F32) - mean
+                go_s[part, :] = (inverse * (qw[part, :].astype(F32) - q_mean - v * projected)).astype(BF16)
         return carry
 
     def feed_back(i, carry):
@@ -567,14 +572,14 @@
         return carry
 
     def forward_sample(b, carry):
-        lax.fori_loop(4 * b, 4 * b + 4, merge_sums, 0)
+        lax.fori_loop(2 * b, 2 * b + 2, merge_sums, 0)
         exchange(b)
         return carry
 
     def backward_sample(b, carry):
         cell_norm(b)
-        lax.fori_loop(4 * b, 4 * b + 4, merge_back, 0)
-        lax.fori_loop(2 * b, 2 * b + 2, feed_back, 0)
+        lax.fori_loop(2 * b, 2 * b + 2, merge_back, 0)
+        feed_back(b, carry)
         return carry
 
     lax.fori_loop(0, 2, forward_sample, 0)
@@ -714,7 +719,7 @@
         def _():
             second_gradients()
 
-        lax.fori_loop(2 * b, 2 * b + 2, project_back, 0)
+        project_back(b, carry)
 
         @pl.when(b == 1)
         def _():

time: 90 us -> 87 us (0.967)
  Pallas kernels: 89.2 us -> 86.1 us
    pallas_call x1, Pallas kernels: 86 us -> 82.9 us  [per_device(): pl.pallas_call(kernel, out_shape=shaped([((TOK, C), BF16), ((2, 8, 64, 38...]
where the time goes in v1:
time: 87 us; the launch traced here: 86.8 us
  Pallas kernels  86.1 us (99%)
    pallas_call x1, Pallas kernels, per_device(): pl.pallas_call(kernel, out_shape=shaped([((TOK, C), BF16), ((2, 8, 64, 38...  82.9 us
    pallas_call x1, Pallas kernels, per_device(): pl.pallas_call(results_kernel, out_shape=shaped([((TOK, C), BF16), ((C, 3...  3.2 us

profile of v1, /device:TPU:1, one launch (start us, length us, event | category | flops | bytes accessed | tf_op | source)
XLA Modules:
  0.0 86.8 jit_solution(11708889415381298416)
XLA Ops:
  0.6 82.9 %shard_map.179 = (bf16[1152,192]{1,0:T(8,128)(2,1)}, bf16[2,8,64,384]{3,2,1,0:T(8,128)(2,1)}, bf16[2,8,96,128]{3,2,1,0:T(8,128)(2,1)}) custom-call(bf16[1152,192]{1,0:T(8,128)(2,1)} %bitcast.18, bf16[576,192]{1,0:T(8,128)(2,1)} %bitcast.19, f32[1,192]{1,0:T(1,128)} %bitcast.23, bf16[192,576]{1,0:T(8,128)(2,1)} %triple_w.3, f32[6,2,3312]{2,1,0:T(2,128)} %bitcast.21, ...), custom_call_target="tpu_custom_call" | custom-call | tf_op jit(solution)/shard_map/pallas_call | solution.py:876
  83.6 3.2 %shard_map.180 = (bf16[1152,192]{1,0:T(8,128)(2,1)}, f32[192,576]{1,0:T(8,128)}, f32[192,192]{1,0:T(8,128)}, f32[192,768]{1,0:T(8,128)}, f32[192,768]{1,0:T(8,12...) custom-call(bf16[1152,192]{1,0:T(8,128)(2,1)} %get-tuple-element.19.fields, ...), custom_call_target="tpu_custom_call" | custom-call | tf_op jit(solution)/shard_map/pallas_call | solution.py:892

commit v2 on v1

--- a/solution.py
+++ b/solution.py
@@ -232,13 +232,10 @@
 
     to_quad = one_hot(HALF, orders[0:1, 0:HALF])
 
-    def sort_sample(b, carry):
-        quads = dot_nn(to_quad, fields[half_rows(b), :])
+    for b in range(2):
+        quads = dot_nn(to_quad, fields[b * HALF:(b + 1) * HALF, :])
         sq[b] = quads
         pack(quads, b, (a10, a01, a11))
-        return carry
-
-    lax.fori_loop(0, 2, sort_sample, 0)
     pl.semaphore_wait(barrier, NCHIP - 1 + NLAT - 1 + 4)
     for b in range(2):
         for copy in rows_ahead(b):
@@ -393,22 +390,20 @@
         return carry
 
 
-    def attend(pair, carry):
-        lw = lax.rem(pair, 2)
-        for i in range(2):
-            rows = window_rows(2 * pair + i)
+    def attend(b):
+        for i in range(4):
+            rows = window_rows(4 * b + i)
             raw[i] = dot_nt(k_s[rows, :], stacked(q_s[rows, :]))
-        for i in range(2):
+        for i in range(4):
             for t in range(WIDE // 128):
                 cols = slice(t * 128, (t + 1) * 128)
-                scores = raw[i, :, cols] * FACTOR + bx[lw, :, cols]
+                scores = raw[i, :, cols] * FACTOR + bx[i // 2, :, cols]
                 exponent = jnp.exp(scores - jnp.max(scores, axis=0, keepdims=True))
                 chances = exponent * (1.0 / jnp.sum(exponent, axis=0, keepdims=True))
-                p_s[2 * pair + i, :, cols] = chances.astype(BF16)
-        for i in range(2):
-            rows = window_rows(2 * pair + i)
-            att_s[rows, :] = per_head(v_s[rows, :], p_s[2 * pair + i]).astype(BF16)
-        return carry
+                p_s[4 * b + i, :, cols] = chances.astype(BF16)
+        for i in range(4):
+            rows = window_rows(4 * b + i)
+            att_s[rows, :] = per_head(v_s[rows, :], p_s[4 * b + i]).astype(BF16)
 
     def forward_windows(b, carry):
         for copy in rows_ahead(b):
@@ -418,7 +413,7 @@
         x_w[half_rows(b), :] = dot_nn(to_window, sq[b].astype(BF16)).astype(BF16)
         project(b, carry)
 
-        lax.fori_loop(2 * b, 2 * b + 2, attend, 0)
+        attend(b)
 
         @pl.when(b == 0)
         def _():
@@ -853,7 +848,7 @@
         vmem(32, 768), vmem(32, 768), vmem(48, 384), vmem(2, 384, 384),
         vmem(12, 128, C), token, vmem(2, WIN, 128, kind=F32), stat, small, small, small, small, vmem(4, WIN, 128, kind=F32),
         token, vmem(TOK, FF), token_f, token, token, vmem(TOK, 768), token,
-        vmem(2, WIN, WIDE, kind=F32), vmem(2, WIN, WIDE), vmem(2, WIDE, C), vmem(CHUNK, FF, kind=F32),
+        vmem(4, WIN, WIDE, kind=F32), vmem(2, WIN, WIDE), vmem(2, WIDE, C), vmem(CHUNK, FF, kind=F32),
         vmem(CHUNK, C, kind=F32),
     ]
     for rows, cols in ((64, 384), (96, 128)):

time: 87 us -> 86.9 us (level)
  no operation moved by 1% of the time
where the time goes in v2:
time: 86.9 us; the launch traced here: 86.8 us
  Pallas kernels  86.1 us (99%)
    pallas_call x1, Pallas kernels, per_device(): pl.pallas_call(kernel, out_shape=shaped([((TOK, C), BF16), ((2, 8, 64, 38...  82.9 us
    pallas_call x1, Pallas kernels, per_device(): pl.pallas_call(results_kernel, out_shape=shaped([((TOK, C), BF16), ((C, 3...  3.2 us

profile of v2, /device:TPU:1, one launch (start us, length us, event | category | flops | bytes accessed | tf_op | source)
XLA Modules:
  0.0 86.8 jit_solution(6270422250830256617)
XLA Ops:
  0.6 82.9 %shard_map.179 = (bf16[1152,192]{1,0:T(8,128)(2,1)}, bf16[2,8,64,384]{3,2,1,0:T(8,128)(2,1)}, bf16[2,8,96,128]{3,2,1,0:T(8,128)(2,1)}) custom-call(bf16[1152,192]{1,0:T(8,128)(2,1)} %bitcast.18, bf16[576,192]{1,0:T(8,128)(2,1)} %bitcast.19, f32[1,192]{1,0:T(1,128)} %bitcast.23, bf16[192,576]{1,0:T(8,128)(2,1)} %triple_w.3, f32[6,2,3312]{2,1,0:T(2,128)} %bitcast.21, ...), custom_call_target="tpu_custom_call" | custom-call | tf_op jit(solution)/shard_map/pallas_call | solution.py:871
  83.6 3.2 %shard_map.180 = (bf16[1152,192]{1,0:T(8,128)(2,1)}, f32[192,576]{1,0:T(8,128)}, f32[192,192]{1,0:T(8,128)}, f32[192,768]{1,0:T(8,128)}, f32[192,768]{1,0:T(8,12...) custom-call(bf16[1152,192]{1,0:T(8,128)(2,1)} %get-tuple-element.19.fields, ...), custom_call_target="tpu_custom_call" | custom-call | tf_op jit(solution)/shard_map/pallas_call | solution.py:887

commit v3 on v2

--- a/solution.py
+++ b/solution.py
@@ -413,18 +413,20 @@
         x_w[half_rows(b), :] = dot_nn(to_window, sq[b].astype(BF16)).astype(BF16)
         project(b, carry)
 
-        attend(b)
-
         @pl.when(b == 0)
         def _():
             arrived(planes.at[:, seven], 1)
             to_band(planes.at[pl.ds(0, 2)], ch, 4, d_dn).start()
 
+        @pl.when(b == 1)
+        def _():
+            arrived(w_all.at[0, seven], 3)
+            to_core(w_all.at[core], w_all.at[core], 16).start()
+
+        attend(b)
         return carry
 
     lax.fori_loop(0, 2, forward_windows, 0)
-    arrived(w_all.at[0, seven], 3)
-    to_core(w_all.at[core], w_all.at[core], 16).start()
 
     def feed(i, carry):
         rows = chunk_rows(i)

time: 86.9 us -> 88.5 us (1.018)
  Pallas kernels: 86.1 us -> 87.7 us
    pallas_call x1, Pallas kernels: 82.9 us -> 84.5 us  [per_device(): pl.pallas_call(kernel, out_shape=shaped([((TOK, C), BF16), ((2, 8, 64, 38...]
where the time goes in v3:
time: 88.5 us; the launch traced here: 88.3 us
  Pallas kernels  87.7 us (99%)
    pallas_call x1, Pallas kernels, per_device(): pl.pallas_call(kernel, out_shape=shaped([((TOK, C), BF16), ((2, 8, 64, 38...  84.5 us
    pallas_call x1, Pallas kernels, per_device(): pl.pallas_call(results_kernel, out_shape=shaped([((TOK, C), BF16), ((C, 3...  3.2 us

profile of v3, /device:TPU:1, one launch (start us, length us, event | category | flops | bytes accessed | tf_op | source)
XLA Modules:
  0.0 88.3 jit_solution(11010846949124580234)
XLA Ops:
  0.6 84.5 %shard_map.179 = (bf16[1152,192]{1,0:T(8,128)(2,1)}, bf16[2,8,64,384]{3,2,1,0:T(8,128)(2,1)}, bf16[2,8,96,128]{3,2,1,0:T(8,128)(2,1)}) custom-call(bf16[1152,192]{1,0:T(8,128)(2,1)} %bitcast.18, bf16[576,192]{1,0:T(8,128)(2,1)} %bitcast.19, f32[1,192]{1,0:T(1,128)} %bitcast.23, bf16[192,576]{1,0:T(8,128)(2,1)} %triple_w.3, f32[6,2,3312]{2,1,0:T(2,128)} %bitcast.21, ...), custom_call_target="tpu_custom_call" | custom-call | tf_op jit(solution)/shard_map/pallas_call | solution.py:873
  85.1 3.2 %shard_map.180 = (bf16[1152,192]{1,0:T(8,128)(2,1)}, f32[192,576]{1,0:T(8,128)}, f32[192,192]{1,0:T(8,128)}, f32[192,768]{1,0:T(8,128)}, f32[192,768]{1,0:T(8,12...) custom-call(bf16[1152,192]{1,0:T(8,128)(2,1)} %get-tuple-element.19.fields, ...), custom_call_target="tpu_custom_call" | custom-call | tf_op jit(solution)/shard_map/pallas_call | solution.py:889
